TPU v7x, 512 devices: a whole 4x4x16 slice. The times are simulated.
512 devices in a mesh: grp: 16 (over y_lo, x, core), rng: 32 (over y_hi, z).
Axes of the slice: x: 4, y: 4 (y_hi: 2, y_lo: 2; y = y_hi * 2 + y_lo), z: 16, core: 2. Of those that a mesh axis runs over, the one named last changes fastest.
Arguments:
- embed: bfloat16 [196608, 1024], P(('grp', 'rng')), may hold values from -72 to 72
- centroids: bfloat16 [4096, 1024], P('grp'), may hold values from -6 to 6
- reach: int32 [196608], P(('grp', 'rng')), may hold values from 1 to 128, as said below
Outputs:
- smoothed: bfloat16 [196608, 1024], P(('grp', 'rng'))
- log_total: float32 [196608], P(('grp', 'rng'))
Inputs may be any that keep to these rules, and one draw needn't show every extreme that they name: Some row has reach exactly 128.
All inputs are finite; a program needn't handle non-finite values.
Results may differ from a plain program's by a relative error of at most 0.0075.
Values may be sent and summed in bfloat16 or wider, within the bound.
A program may use at most 64 MiB of HBM per device.

v0:
```python
import jax
import jax.numpy as jnp
from jax import lax
from jax.sharding import PartitionSpec as P

HALO = 128


logit_gain = 3.0


def padded(value, sides, width):
    for axis, dim in sides:
        size, length = (lax.axis_size(axis), value.shape[dim])
        up = [(i, (i + 1) % size) for i in range(size)]
        down = [(j, i) for i, j in up]
        last = lax.slice_in_dim(value, length - width, length, axis=dim)
        initial = lax.slice_in_dim(value, 0, width, axis=dim)
        before = lax.ppermute(last, axis, up)
        after = lax.ppermute(initial, axis, down)
        value = jnp.concatenate([before, value, after], axis=dim)
    return value


def make_step(rows):
    gain = logit_gain / jnp.sqrt(jnp.float32(rows.shape[1]))

    def step(carry, piece, start):
        top, total, accum = carry
        score = (
            lax.dot_general(
                rows, piece, (((1,), (1,)), ((), ())), preferred_element_type=jnp.float32
            )
            * gain
        )
        new_top = jnp.maximum(top, jnp.max(score, axis=1))
        expo = jnp.exp(score - new_top[:, None])
        total = jnp.sum(expo, axis=1)
        accum = jnp.dot(expo.astype(jnp.bfloat16), piece, preferred_element_type=jnp.float32)
        return (new_top, total, accum)

    return step


def assign(rows, centroids):
    count = rows.shape[0]
    start_carry = (
        jnp.full((count,), -1e30, jnp.float32),
        jnp.zeros((count,), jnp.float32),
        jnp.zeros((count, rows.shape[1]), jnp.float32),
    )
    step = make_step(rows)
    top, total, accum = step(
        start_carry, lax.all_gather(centroids, "grp", axis=0, tiled=True), jnp.int32(0)
    )
    assigned = (accum / total[:, None]).astype(jnp.bfloat16)
    return (assigned, top + jnp.log(total))


def smooth(local, reach_rows, ext_rows, ext_assigned, margin):
    band = lax.dot_general(
        local, ext_rows, (((1,), (1,)), ((), ())), preferred_element_type=jnp.float32
    ) / jnp.sqrt(jnp.float32(local.shape[1]))
    offset = jnp.arange(ext_rows.shape[0], dtype=jnp.int32)[None, :] - (
        jnp.arange(local.shape[0], dtype=jnp.int32)[:, None] + margin
    )
    inside = (jnp.abs(offset) <= reach_rows[:, None]) & (offset != 0)
    band = jnp.where(inside, band, jnp.float32(-1e30))
    peak = jnp.max(band, axis=1)
    expo = jnp.where(inside, jnp.exp(band - peak[:, None]), jnp.float32(0.0))
    mix = (expo / jnp.sum(expo, axis=1)[:, None]).astype(jnp.bfloat16)
    return jnp.dot(mix, ext_assigned, preferred_element_type=jnp.float32).astype(jnp.bfloat16)


def shards(embed, centroids, reach):
    assigned, log_total = assign(embed, centroids)
    stacked = jnp.stack([embed, assigned], axis=0)
    extended = padded(stacked, (("rng", 1),), HALO)
    ext_rows = extended[0]
    ext_assigned = extended[1]
    smoothed = smooth(embed, reach, ext_rows, ext_assigned, HALO)
    return (smoothed, log_total)


def solution(mesh):
    return jax.shard_map(
        shards,
        mesh=mesh,
        in_specs=(P(("grp", "rng"), None), P("grp", None), P(("grp", "rng"))),
        out_specs=(P(("grp", "rng"), None), P(("grp", "rng"))),
        check_vma=False,
    )
```

profile of v0, /device:TPU:1, one launch (start us, length us, event | category | flops | bytes accessed | tf_op | source)
XLA Modules:
  0.0 118.5 jit_solution(15542985725026790786)
XLA Ops:
  7.2 0.0 all-gather.2.cloned.1.call-start
  7.2 0.7 all-gather.2.cloned.1.call-update
  7.9 67.8 %all-gather.2.cloned.1.call-done = bf16[4096,1024]{1,0:T(8,128)(2,1)} async-done(((bf16[256,1024]{1,0:T(8,128)(2,1)}), bf16[4096,1024]{1,0:T(8,128)(2,1)}) %all-gather.2.cloned.1.call-update) | async-done | bytes 8388624 | tf_op jit(solution)/shard_map/all_gather | solution.py:54
  75.7 0.0 copy-start.2
  75.7 6.8 %fusion.21 = (f32[384]{0:T(512)S(1)}, f32[384,4096]{1,0:T(8,128)S(1)}) fusion(bf16[384,1024]{1,0:T(8,128)(2,1)} %param.3, bf16[4096,1024]{1,0:T(8,128)(2,1)} %all-gather.2.cloned.1.call-done), kind=kOutput, calls=%fused_computation.32 | convolution fusion | flops 3224370688 | bytes 15468032 | tf_op jit(solution)/shard_map/dot_general | solution.py:31
  82.5 1.0 fusion
  83.5 0.0 copy-done.2
  83.5 0.0 copy-start
  83.5 3.5 %fusion.9 = bf16[1,384,1024]{2,1,0:T(8,128)(2,1)S(1)} fusion(bf16[4096,1024]{1,0:T(8,128)(2,1)S(1)} %copy-done.2, f32[384,4096]{1,0:T(8,128)S(1)} %get-tuple-element.5, f32[384]{0:T(512)S(1)} %broadcast_maximum_fusion, f32[384]{0:T(512)S(1)} %fusion), kind=kOutput, calls=%fused_computation.14 | convolution fusion | flops 3225157632 | bytes 15469568 | tf_op jit(solution)/shard_map/dot_general | solution.py:39
  87.0 0.0 copy-start.1
  87.0 0.0 copy-done
  87.0 0.1 pad_maximum_fusion.2
  87.1 3.2 %collective-permute-start = (bf16[2,128,1024]{2,1,0:T(8,128)(2,1)S(1)}, bf16[2,128,1024]{2,1,0:T(8,128)(2,1)S(1)}, u32[]{:S(2)}, u32[]{:S(2)}) collective-permute-start(bf16[2,128,1024]{2,1,0:T(8,128)(2,1)S(1)} %get-tuple-element.2), channel_id=1, source_target_pairs={{0,1},{1,2},{2,3},{3,4},{4,5},{5,6},{6,7},{7,8},{8,9},{9,10},{10,1... | collective-permute-start | bytes 1572872 | tf_op jit(solution)/shard_map/ppermute | solution.py:19
  90.3 6.8 %collective-permute-start.1 = (bf16[2,128,1024]{2,1,0:T(8,128)(2,1)S(1)}, bf16[2,128,1024]{2,1,0:T(8,128)(2,1)S(1)}, u32[]{:S(2)}, u32[]{:S(2)}) collective-permute-start(bf16[2,128,1024]{2,1,0:T(8,128)(2,1)S(1)} %get-tuple-element.3), channel_id=1, source_target_pairs={{1,0},{2,1},{3,2},{4,3},{5,4},{6,5},{7,6},{8,7},{9,8},{10,9},{11,1... | collective-permute-start | bytes 1572872 | tf_op jit(solution)/shard_map/ppermute | solution.py:20
  97.0 0.6 log_add_fusion
  97.6 9.6 %collective-permute-done = bf16[2,128,1024]{2,1,0:T(8,128)(2,1)S(1)} collective-permute-done((bf16[2,128,1024]{2,1,0:T(8,128)(2,1)S(1)}, bf16[2,128,1024]{2,1,0:T(8,128)(2,1)S(1)}, u32[]{:S(2)}, u32[]{:S(2)}) %collective-permute-start) | collective-permute-done | bytes 524320 | tf_op jit(solution)/shard_map/ppermute | solution.py:19
  107.2 0.9 collective-permute-done.1
  108.0 0.3 pad_maximum_fusion
  108.4 0.0 copy-done.1
  108.4 1.0 fusion.22
  109.4 0.4 fusion.14
  109.8 1.9 %convolution_convert_fusion = bf16[384,1024]{1,0:T(8,128)(2,1)} fusion(bf16[2,640,1024]{2,1,0:T(8,128)(2,1)S(1)} %pad_maximum_fusion, f32[384,640]{0,1:T(8,128)S(1)} %get-tuple-element.7, f32[384]{0:T(512)S(1)} %fusion.14, f32[384]{0:T(512)S(1)} %get-tuple-element.6, s32[384]{0:T(512)S(1)} %copy-done.1, s32[384]{0:T(512)S(1)} %iota_add_fusion), kind=kOutput, calls=%fused_computation.8 | convolution fusion | flops 505921536 | bytes 3088384 | tf_op jit(solution)/shard_map/dot_general | solution.py:72
  (2 shorter events, 0.0 us)
Async XLA Ops:
  7.2 68.5 %all-gather.2.cloned.1.call-start = ((), (), s32[]{:S(2)}) async-start(), calls=%async_computation | async-start | bytes 8912896 | tf_op jit(solution)/shard_map/all_gather | solution.py:54
  75.7 7.8 %copy-start.2 = (bf16[4096,1024]{1,0:T(8,128)(2,1)S(1)}, bf16[4096,1024]{1,0:T(8,128)(2,1)}, u32[]{:S(2)}) copy-start(bf16[4096,1024]{1,0:T(8,128)(2,1)} %all-gather.2.cloned.1.call-done) | copy-start | bytes 25165828
  83.5 3.5 %copy-start = (bf16[384,1024]{1,0:T(8,128)(2,1)S(1)}, bf16[384,1024]{1,0:T(8,128)(2,1)}, u32[]{:S(2)}) copy-start(bf16[384,1024]{1,0:T(8,128)(2,1)} %param.3) | copy-start | bytes 2359300
  87.0 21.4 %copy-start.1 = (s32[384]{0:T(512)S(1)}, s32[384]{0:T(512)}, u32[]{:S(2)}) copy-start(s32[384]{0:T(512)} %param.5) | copy-start | bytes 4612
  87.1 20.1 %collective-permute-start = (bf16[2,128,1024]{2,1,0:T(8,128)(2,1)S(1)}, bf16[2,128,1024]{2,1,0:T(8,128)(2,1)S(1)}, u32[]{:S(2)}, u32[]{:S(2)}) collective-permute-start(bf16[2,128,1024]{2,1,0:T(8,128)(2,1)S(1)} %get-tuple-element.2), channel_id=1, source_target_pairs={{0,1},{1,2},{2,3},{3,4},{4,5},{5,6},{6,7},{7,8},{8,9},{9,10},{10,1... | collective-permute-start | bytes 1572872 | tf_op jit(solution)/shard_map/ppermute | solution.py:19
  90.3 17.8 %collective-permute-start.1 = (bf16[2,128,1024]{2,1,0:T(8,128)(2,1)S(1)}, bf16[2,128,1024]{2,1,0:T(8,128)(2,1)S(1)}, u32[]{:S(2)}, u32[]{:S(2)}) collective-permute-start(bf16[2,128,1024]{2,1,0:T(8,128)(2,1)S(1)} %get-tuple-element.3), channel_id=1, source_target_pairs={{1,0},{2,1},{3,2},{4,3},{5,4},{6,5},{7,6},{8,7},{9,8},{10,9},{11,1... | collective-permute-start | bytes 1572872 | tf_op jit(solution)/shard_map/ppermute | solution.py:20
Sparse Core Ops, SparseCore 0:
  10.1 65.4 all-gather.1
where the time goes:
time: 119 us
  waiting for transfers between devices  78.9 us (66%)
  between operations  14.1 us (12%)
  matrix products  13.2 us (11%)
  starting transfers between devices  9.98 us (8%)
  other arithmetic  2.37 us (2%)
    all_gather x1, waiting for transfers between devices, assign(): lax.all_gather(centroids, 'grp', axis=0, tiled=True)  67.8 us
    ppermute x1, waiting for transfers between devices, padded(): before = lax.ppermute(last, axis, up)  9.57 us
    dot_general x1, matrix products, step(): lax.dot_general(rows, piece, (((1,), (1,)), ((), ())), preferred_element_...  6.79 us
    ppermute x1, starting transfers between devices, padded(): after = lax.ppermute(initial, axis, down)  6.76 us
    dot_general x1, matrix products, step(): jnp.dot(expo.astype(jnp.bfloat16), piece, preferred_element_type=jnp.floa...  3.46 us
    ppermute x1, starting transfers between devices, padded(): before = lax.ppermute(last, axis, up)  3.18 us
  transfers between devices with their start and end apart: 3, of which 3 were waited for; matrix products, arithmetic and copies ran while one was open for 0% of the time, Pallas kernels for 0%

commit v1 on v0

v1 whole, which is shorter than its diff:
```python
import functools

import jax
import jax.numpy as jnp
from jax import lax
from jax.experimental import pallas as pl
from jax.experimental.pallas import tpu as pltpu
from jax.sharding import PartitionSpec as P

HALO = 128
MESH = pl.DeviceIdType.MESH
LOG2E = 1.4426950408889634
LN2 = 0.6931471805599453

SCHEDULE = (
    {"x+": "D0", "x-": "D1", "ya": "D0", "yb": "D1"},
    {"x+": "D1", "x-": "D0", "ya": "n0", "yb": "n1"},
    {
        "x+": (0, "x+"),
        "x-": (0, "x-"),
        "ya": (0, "x+"),
        "yb": (0, "x-"),
        "z+": (0, "x+"),
        "z-": (0, "x-"),
    },
    {
        "x+": (1, "yb"),
        "x-": (1, "ya"),
        "ya": (1, "x-"),
        "yb": (1, "x+"),
        "z+": (1, "x-"),
        "z-": (1, "x+"),
    },
    {"x+": (2, "ya"), "x-": (2, "yb"), "z+": (2, "ya"), "z-": (2, "yb")},
    {"x+": (3, "x+"), "x-": (3, "x-"), "z+": (2, "x+"), "z-": (2, "x-")},
)
N_SLOT = len(SCHEDULE)


def neighbours():
    g, r = lax.axis_index("grp"), lax.axis_index("rng")
    n_rng = lax.axis_size("rng")
    n_z = n_rng // 2
    core, x, y_lo = lax.rem(g, 2), lax.rem(g // 2, 4), g // 8
    z, y_hi = lax.rem(r, n_z), r // n_z

    def grp(xx, yy, cc):
        return (yy * 4 + xx) * 2 + cc

    across = grp(x, 1 - y_lo, core)
    return {
        "x+": (grp(lax.rem(x + 1, 4), y_lo, core), r),
        "x-": (grp(lax.rem(x + 3, 4), y_lo, core), r),
        "ya": (across, r),
        "yb": (across, (1 - y_hi) * n_z + z),
        "z+": (g, y_hi * n_z + lax.rem(z + 1, n_z)),
        "z-": (g, y_hi * n_z + lax.rem(z + n_z - 1, n_z)),
        "sib": (grp(x, y_lo, 1 - core), r),
        "next": (g, lax.rem(r + 1, n_rng)),
        "prev": (g, lax.rem(r + n_rng - 1, n_rng)),
    }, lax.rem(z, 2)


def kernel(
    embed, cent, reach, out, lse, rows, table, acc, peak, part, mix,
    ici_send, ici_recv, sib_send, sib_recv, halo_send, halo_recv, own_sem,
):
    count, width = embed.shape
    block = cent.shape[0]
    quarter = block // 4
    total_rows = count + 2 * HALO
    gain = 3.0 / (width**0.5)
    to_exp2 = gain * LOG2E
    nbr, parity = neighbours()

    barrier = pltpu.get_barrier_semaphore()
    for device in nbr.values():
        pl.semaphore_signal(barrier, inc=1, device_id=device, device_id_type=MESH)

    load_rows = pltpu.make_async_copy(embed, rows.at[pl.ds(0, count)], own_sem.at[0])
    load_own = pltpu.make_async_copy(cent, table.at[pl.ds(0, block)], own_sem.at[1])
    load_rows.start()
    load_own.start()

    base, pieces = [], []
    at = 2 * block
    for slot in SCHEDULE:
        base.append(at)
        pieces.append(list(slot))
        at += 2 * len(slot) * quarter

    def landing(slot, link):
        return pl.ds(base[slot] + pieces[slot].index(link) * quarter, quarter)

    def source(what):
        if isinstance(what, tuple):
            return table.at[landing(*what)]
        half = parity if what[0] == "D" else 1 - parity
        start = pl.multiple_of(half * (2 * quarter) + int(what[1]) * quarter, quarter)
        return cent.at[pl.ds(start, quarter)]

    def ici(slot, link):
        index = list(SCHEDULE[3]).index(link)
        return pltpu.make_async_remote_copy(
            src_ref=source(SCHEDULE[slot][link]),
            dst_ref=table.at[landing(slot, link)],
            send_sem=ici_send.at[slot, index],
            recv_sem=ici_recv.at[slot, index],
            device_id=nbr[link],
            device_id_type=MESH,
        )

    def share(slot):
        if slot < 0:
            src, dst = cent, table.at[pl.ds(block, block)]
        else:
            size = len(pieces[slot]) * quarter
            src = table.at[pl.ds(base[slot], size)]
            dst = table.at[pl.ds(base[slot] + size, size)]
        return pltpu.make_async_remote_copy(
            src_ref=src,
            dst_ref=dst,
            send_sem=sib_send.at[slot + 1],
            recv_sem=sib_recv.at[slot + 1],
            device_id=nbr["sib"],
            device_id_type=MESH,
        )

    copies = [{link: ici(s, link) for link in pieces[s]} for s in range(N_SLOT)]
    shares = [share(s) for s in range(-1, N_SLOT)]
    halo = [
        pltpu.make_async_remote_copy(
            src_ref=embed.at[pl.ds(count - HALO, HALO)],
            dst_ref=rows.at[pl.ds(count, HALO)],
            send_sem=halo_send.at[0],
            recv_sem=halo_recv.at[0],
            device_id=nbr["next"],
            device_id_type=MESH,
        ),
        pltpu.make_async_remote_copy(
            src_ref=embed.at[pl.ds(0, HALO)],
            dst_ref=rows.at[pl.ds(count + HALO, HALO)],
            send_sem=halo_send.at[1],
            recv_sem=halo_recv.at[1],
            device_id=nbr["prev"],
            device_id_type=MESH,
        ),
    ]

    pl.semaphore_wait(barrier, len(nbr))
    for copy in copies[0].values():
        copy.start()
    for copy in halo:
        copy.start()
    shares[0].start()
    for copy in copies[1].values():
        copy.start()

    def score(r, n, c, k):
        return lax.dot_general(
            rows[pl.ds(r, n), :],
            table[pl.ds(c, k), :],
            (((1,), (1,)), ((), ())),
            preferred_element_type=jnp.float32,
        )

    def absorb(s, r, n, c, k, first):
        top = jnp.broadcast_to(jnp.max(s, axis=1, keepdims=True), (n, 128))
        if not first:
            old = peak[pl.ds(r, n), :]
            top = jnp.maximum(old, top)
            scale = jnp.exp2((old - top) * to_exp2)
        weight = jnp.exp2((s - top[:, :1]) * to_exp2)
        lanes = weight[:, :128]
        for j in range(1, k // 128):
            lanes = lanes + weight[:, j * 128 : (j + 1) * 128]
        peak[pl.ds(r, n), :] = top
        value = jnp.dot(
            weight.astype(jnp.bfloat16),
            table[pl.ds(c, k), :],
            preferred_element_type=jnp.float32,
        )
        if first:
            part[pl.ds(r, n), :] = lanes
            acc[pl.ds(r, n), :] = value
        else:
            part[pl.ds(r, n), :] = part[pl.ds(r, n), :] * scale + lanes
            acc[pl.ds(r, n), :] = acc[pl.ds(r, n), :] * scale[:, :1] + value

    def work(units):
        s = score(*units[0][:4])
        for i, unit in enumerate(units):
            later = score(*units[i + 1][:4]) if i + 1 < len(units) else None
            absorb(s, *unit)
            s = later

    def halves(r, n, c, k, first=False):
        return [(r, n // 2, c, k, first), (r + n // 2, n // 2, c, k, first)]

    load_rows.wait()
    load_own.wait()
    shares[0].wait_recv()
    work(halves(0, count, 0, 2 * block, True))

    for slot in range(N_SLOT):
        for copy in copies[slot].values():
            copy.wait_recv()
        shares[slot + 1].start()
        if slot + 2 < N_SLOT:
            for copy in copies[slot + 2].values():
                copy.start()
        size = 2 * len(pieces[slot]) * quarter
        if slot == 1:
            for copy in halo:
                copy.wait_recv()
            work([(count, 2 * HALO, 0, 2 * block, True), (count, 2 * HALO, base[0], base[1] - base[0], False)])
        if slot == 4:
            band = lax.dot_general(
                rows[pl.ds(0, count), :],
                rows[...],
                (((1,), (1,)), ((), ())),
                preferred_element_type=jnp.float32,
            )
            band = band * (1.0 / width**0.5)
            column = lax.broadcasted_iota(jnp.int32, (count, total_rows), 1)
            place = column - jnp.where(
                column < count, 0, jnp.where(column < count + HALO, count + HALO, HALO)
            )
            offset = place - lax.broadcasted_iota(jnp.int32, (count, total_rows), 0)
            inside = (jnp.abs(offset) <= reach[...]) & (offset != 0)
            band = jnp.where(inside, band, jnp.float32(-1e30))
            highest = jnp.max(band, axis=1, keepdims=True)
            expo = jnp.where(inside, jnp.exp(band - highest), jnp.float32(0.0))
            mix[...] = (expo / jnp.sum(expo, axis=1, keepdims=True)).astype(jnp.bfloat16)
        shares[slot + 1].wait_recv()
        if slot == 0:
            work(halves(0, count, base[slot], size))
        else:
            work(halves(0, total_rows, base[slot], size))

    total = jnp.sum(part[...], axis=1, keepdims=True)
    assigned = (acc[...] / total).astype(jnp.bfloat16)
    lse[...] = peak[pl.ds(0, count), :1] * gain + jnp.log(total[:count])
    out[...] = jnp.dot(mix[...], assigned, preferred_element_type=jnp.float32).astype(
        jnp.bfloat16
    )

    for slot in range(N_SLOT):
        for copy in copies[slot].values():
            copy.wait_send()
    for copy in shares + halo:
        copy.wait_send()


def shards(embed, centroids, reach):
    count, width = embed.shape
    block = centroids.shape[0]
    total = count + 2 * HALO
    table = block * lax.axis_size("grp")
    vmem = pl.BlockSpec(memory_space=pltpu.VMEM)
    hbm = pl.BlockSpec(memory_space=pl.ANY)
    smoothed, log_total = pl.pallas_call(
        kernel,
        out_shape=(
            jax.ShapeDtypeStruct((count, width), jnp.bfloat16),
            jax.ShapeDtypeStruct((count, 1), jnp.float32),
        ),
        in_specs=[hbm, hbm, vmem],
        out_specs=(vmem, vmem),
        scratch_shapes=[
            pltpu.VMEM((total, width), jnp.bfloat16),
            pltpu.VMEM((table, width), jnp.bfloat16),
            pltpu.VMEM((total, width), jnp.float32),
            pltpu.VMEM((total, 128), jnp.float32),
            pltpu.VMEM((total, 128), jnp.float32),
            pltpu.VMEM((count, total), jnp.bfloat16),
            pltpu.SemaphoreType.DMA((N_SLOT, 6)),
            pltpu.SemaphoreType.DMA((N_SLOT, 6)),
            pltpu.SemaphoreType.DMA((N_SLOT + 1,)),
            pltpu.SemaphoreType.DMA((N_SLOT + 1,)),
            pltpu.SemaphoreType.DMA((2,)),
            pltpu.SemaphoreType.DMA((2,)),
            pltpu.SemaphoreType.DMA((2,)),
        ],
        compiler_params=pltpu.CompilerParams(
            collective_id=0, has_side_effects=True, vmem_limit_bytes=48 * 2**20
        ),
        cost_estimate=pl.CostEstimate(
            flops=4 * total * table * width, bytes_accessed=8 * 2**20, transcendentals=total * table
        ),
    )(embed, centroids, reach[:, None])
    return smoothed, log_total[:, 0]


def solution(mesh):
    return jax.shard_map(
        shards,
        mesh=mesh,
        in_specs=(P(("grp", "rng"), None), P("grp", None), P(("grp", "rng"))),
        out_specs=(P(("grp", "rng"), None), P(("grp", "rng"))),
        check_vma=False,
    )
```

time: 119 us -> 54.1 us (0.45)
  waiting for transfers between devices: 78.9 us -> 0 us
  Pallas kernels: 0 us -> 48.7 us
  between operations: 14.1 us -> 0.66 us
  matrix products: 13.2 us -> 0 us
  starting transfers between devices: 9.98 us -> 0 us
  local copies, waits for them, and re-layouts: 0.02 us -> 3.84 us
  other arithmetic: 2.37 us -> 0.73 us
    all_gather x1 -> x0, waiting for transfers between devices: 67.8 us -> none  [assign(): lax.all_gather(centroids, 'grp', axis=0, tiled=True)]
    pallas_call x0 -> x1, Pallas kernels: none -> 48.7 us  [shards(): pl.pallas_call(kernel, out_shape=(jax.ShapeDtypeStruct((count, width), jn...]
    dot_general x4 -> x0, matrix products: 13.2 us -> none  [the longest x1 6.79 us: step(): lax.dot_general(rows, piece, (((1,), (1,)), ((), ())), preferred_element_...]
    ppermute x2 -> x0, waiting for transfers between devices: 10.4 us -> none  [the longest x1 9.57 us: padded(): before = lax.ppermute(last, axis, up)]
    ppermute x2 -> x0, starting transfers between devices: 9.94 us -> none  [the longest x1 6.76 us: padded(): after = lax.ppermute(initial, axis, down)]
    unnamed x6 -> x5, local copies, waits for them, and re-layouts: 0.02 us -> 3.05 us
    reduce_sum x2 -> x0, other arithmetic: 1.4 us -> none  [the longest x1 0.98 us: step(): total = jnp.sum(expo, axis=1)]
  transfers between devices with their start and end apart: 3 -> 0, of which waited for: 3 -> 0; matrix products, arithmetic and copies ran while one was open for 0% -> 0% of each run, Pallas kernels for 0% -> 0%
where the time goes in v1:
time: 54.1 us; the launch traced here: 53.9 us
  Pallas kernels  48.7 us (90%)
  local copies, waits for them, and re-layouts  3.84 us (7%)
  other arithmetic  0.73 us (1%)
  between operations  0.66 us (1%)
    pallas_call x1, Pallas kernels, shards(): pl.pallas_call(kernel, out_shape=(jax.ShapeDtypeStruct((count, width), jn...  48.7 us
    unnamed x5, local copies, waits for them, and re-layouts  3.05 us

profile of v1, /device:TPU:1, one launch (start us, length us, event | category | flops | bytes accessed | tf_op | source)
XLA Modules:
  0.0 53.9 jit_solution(6680382423276156043)
XLA Ops:
  0.6 0.8 %broadcast_in_dim.4.reach = s32[384,1]{1,0:T(8,128)S(1)} reshape(s32[384]{0:T(512)} %param.5) | data formatting | bytes 3072 | tf_op jit(solution)/shard_map/broadcast_in_dim | solution.py:291
  1.4 0.0 copy-start
  1.4 1.1 %copy-done = bf16[384,1024]{1,0:T(8,128)(2,1)S(1)} copy-done((bf16[384,1024]{1,0:T(8,128)(2,1)S(1)}, bf16[384,1024]{1,0:T(8,128)(2,1)}, u32[]{:S(2)}) %copy-start) | copy-done | bytes 786456
  2.6 0.0 copy-start.1
  2.6 1.0 %copy-done.1 = bf16[256,1024]{1,0:T(8,128)(2,1)S(1)} copy-done((bf16[256,1024]{1,0:T(8,128)(2,1)S(1)}, bf16[256,1024]{1,0:T(8,128)(2,1)}, u32[]{:S(2)}) %copy-start.1) | copy-done | bytes 524312
  3.6 48.7 %shard_map.50 = (bf16[384,1024]{1,0:T(8,128)(2,1)S(1)}, f32[384,1]{1,0:T(8,128)S(1)}) custom-call(bf16[384,1024]{1,0:T(8,128)(2,1)S(1)} %copy-done, bf16[256,1024]{1,0:T(8,128)(2,1)S(1)} %copy-done.1, s32[384,1]{1,0:T(8,128)S(1)} %broadcast_in_dim.4.reach), custom_call_target="tpu_custom_call" | custom-call | flops 10737418240 | bytes 8388608 | tf_op jit(solution)/shard_map/pallas_call | solution.py:262
  52.3 0.7 %reduce = f32[384]{0:T(512)} reduce(f32[384,1]{1,0:T(8,128)S(1)} %get-tuple-element.5, f32[]{:T(128)} %constant.2), dimensions={1}, to_apply=%get-tuple-element.5.reduce_sub_computation | reduce | bytes 3076 | tf_op jit(solution)/shard_map/pallas_call | solution.py:262
  53.0 0.9 %copy.7 = bf16[384,1024]{1,0:T(8,128)(2,1)} copy(bf16[384,1024]{1,0:T(8,128)(2,1)S(1)} %get-tuple-element.8) | data formatting | bytes 1572864
Async XLA Ops:
  1.4 1.1 %copy-start = (bf16[384,1024]{1,0:T(8,128)(2,1)S(1)}, bf16[384,1024]{1,0:T(8,128)(2,1)}, u32[]{:S(2)}) copy-start(bf16[384,1024]{1,0:T(8,128)(2,1)} %embed.1) | copy-start | bytes 2359300
  2.6 1.0 %copy-start.1 = (bf16[256,1024]{1,0:T(8,128)(2,1)S(1)}, bf16[256,1024]{1,0:T(8,128)(2,1)}, u32[]{:S(2)}) copy-start(bf16[256,1024]{1,0:T(8,128)(2,1)} %cent.1) | copy-start | bytes 1572868

commit v2 on v1

v2 whole, which is shorter than its diff:
```python
import functools

import jax
import jax.numpy as jnp
from jax import lax
from jax.experimental import pallas as pl
from jax.experimental.pallas import tpu as pltpu
from jax.sharding import PartitionSpec as P

HALO = 128
MESH = pl.DeviceIdType.MESH
LOG2E = 1.4426950408889634
LN2 = 0.6931471805599453

SECOND = -1
SENDS = (
    ("p1", "x+", "D0", 0, 1),
    ("m1", "x-", "D1", 0, 1),
    ("a1", "ya", "n0", 0, 2),
    ("b1", "yb", "n1", 0, 2),
    ("p2", "x+", "D1", SECOND, 2),
    ("m2", "x-", "D0", SECOND, 2),
    ("p3", "x+", "p1", 1, 3),
    ("m3", "x-", "m1", 1, 3),
    ("u1", "z+", "p1", 1, 3),
    ("d1", "z-", "m1", 1, 3),
    ("a2", "ya", "p1", 1, 4),
    ("b2", "yb", "m1", 1, 4),
    ("p4", "x+", "b1", 2, 4),
    ("m4", "x-", "a1", 2, 4),
    ("u2", "z+", "m2", 2, 4),
    ("d2", "z-", "p2", 2, 4),
    ("a3", "ya", "m2", 2, 5),
    ("b3", "yb", "p2", 2, 5),
    ("u3", "z+", "p3", 3, 5),
    ("d3", "z-", "m3", 3, 5),
    ("a4", "ya", "D0", 3, 6),
    ("b4", "yb", "D1", 3, 6),
    ("p5", "x+", "p4", 4, 5),
    ("m5", "x-", "m4", 4, 5),
    ("u4", "z+", "a2", 4, 7),
    ("d4", "z-", "b2", 4, 7),
    ("p6", "x+", "a2", 4, 7),
    ("m6", "x-", "b2", 4, 7),
)
GROUPS = (
    (1, ("p1", "m1")),
    (2, ("p2", "m2", "a1", "b1")),
    (3, ("p3", "m3", "u1", "d1")),
    (4, ("p4", "m4", "u2", "d2")),
    (5, ("p5", "m5", "u3", "d3")),
    (5, ("a2", "b2", "a3", "b3")),
    (6, ("a4", "b4")),
    (7, ("p6", "m6", "u4", "d4")),
)


def neighbours():
    g, r = lax.axis_index("grp"), lax.axis_index("rng")
    n_rng = lax.axis_size("rng")
    n_z = n_rng // 2
    core, x, y_lo = lax.rem(g, 2), lax.rem(g // 2, 4), g // 8
    z, y_hi = lax.rem(r, n_z), r // n_z

    def grp(xx, yy, cc):
        return (yy * 4 + xx) * 2 + cc

    across = grp(x, 1 - y_lo, core)
    return {
        "x+": (grp(lax.rem(x + 1, 4), y_lo, core), r),
        "x-": (grp(lax.rem(x + 3, 4), y_lo, core), r),
        "ya": (across, r),
        "yb": (across, (1 - y_hi) * n_z + z),
        "z+": (g, y_hi * n_z + lax.rem(z + 1, n_z)),
        "z-": (g, y_hi * n_z + lax.rem(z + n_z - 1, n_z)),
        "sib": (grp(x, y_lo, 1 - core), r),
        "next": (g, lax.rem(r + 1, n_rng)),
        "prev": (g, lax.rem(r + n_rng - 1, n_rng)),
    }, lax.rem(z, 2)


def kernel(
    embed, cent, reach_in, out, lse, rows, table, acc, peak, part, band, mix, assigned, reach,
    ici_send, ici_recv, sib_send, sib_recv, halo_send, halo_recv, own_sem,
):
    count, width = embed.shape
    block = cent.shape[0]
    quarter = block // 4
    total_rows = count + 2 * HALO
    gain = 3.0 / (width**0.5)
    to_exp2 = gain * LOG2E
    nbr, parity = neighbours()

    barrier = pltpu.get_barrier_semaphore()
    for device in nbr.values():
        pl.semaphore_signal(barrier, inc=1, device_id=device, device_id_type=MESH)

    load_rows = pltpu.make_async_copy(embed, rows.at[pl.ds(0, count)], own_sem.at[0])
    load_own = pltpu.make_async_copy(cent, table.at[pl.ds(0, block)], own_sem.at[1])
    load_reach = pltpu.make_async_copy(reach_in, reach, own_sem.at[2])
    load_rows.start()
    load_reach.start()
    load_own.start()

    place, base, size = {}, [0], [block]
    for _, names in GROUPS:
        base.append(base[-1] + 2 * size[-1])
        size.append(len(names) * quarter)
        for i, name in enumerate(names):
            place[name] = pl.ds(base[-1] + i * quarter, quarter)

    def source(what):
        if what in place:
            return table.at[place[what]]
        half = parity if what[0] == "D" else 1 - parity
        start = pl.multiple_of(half * (2 * quarter) + int(what[1]) * quarter, quarter)
        return cent.at[pl.ds(start, quarter)]

    copies = []
    for i, (name, link, what, _, _) in enumerate(SENDS):
        copies.append(
            pltpu.make_async_remote_copy(
                src_ref=source(what),
                dst_ref=table.at[place[name]],
                send_sem=ici_send.at[i],
                recv_sem=ici_recv.at[i],
                device_id=nbr[link],
                device_id_type=MESH,
            )
        )
    shares = [
        pltpu.make_async_remote_copy(
            src_ref=cent if group == 0 else table.at[pl.ds(base[group], size[group])],
            dst_ref=table.at[pl.ds(base[group] + size[group], size[group])],
            send_sem=sib_send.at[group],
            recv_sem=sib_recv.at[group],
            device_id=nbr["sib"],
            device_id_type=MESH,
        )
        for group in range(len(GROUPS) + 1)
    ]
    halo = [
        pltpu.make_async_remote_copy(
            src_ref=embed.at[pl.ds(start, HALO)],
            dst_ref=rows.at[pl.ds(count + side * HALO, HALO)],
            send_sem=halo_send.at[side],
            recv_sem=halo_recv.at[side],
            device_id=nbr[to],
            device_id_type=MESH,
        )
        for side, (start, to) in enumerate(((count - HALO, "next"), (0, "prev")))
    ]

    def launch(slot):
        for send, copy in zip(SENDS, copies):
            if send[3] == slot:
                copy.start()

    def boundary(slot):
        for send, copy in zip(SENDS, copies):
            if send[4] == slot:
                copy.wait_recv()
        launch(slot)
        for group, (ready, _) in enumerate(((0, ()), *GROUPS)):
            if ready == slot:
                shares[group].start()
        if slot == 0:
            for copy in halo:
                copy.start()

    def score(r, n, c, k):
        return lax.dot_general(
            rows[pl.ds(r, n), :],
            table[pl.ds(c, k), :],
            (((1,), (1,)), ((), ())),
            preferred_element_type=jnp.float32,
        )

    def absorb(s, r, n, c, k, first):
        top = jnp.broadcast_to(jnp.max(s, axis=1, keepdims=True), (n, 128))
        if not first:
            old = peak[pl.ds(r, n), :]
            top = jnp.maximum(old, top)
            scale = jnp.exp2((old - top) * to_exp2)
        weight = jnp.exp2((s - top[:, :1]) * to_exp2)
        lanes = weight[:, :128]
        for j in range(1, k // 128):
            lanes = lanes + weight[:, j * 128 : (j + 1) * 128]
        peak[pl.ds(r, n), :] = top
        value = jnp.dot(
            weight.astype(jnp.bfloat16),
            table[pl.ds(c, k), :],
            preferred_element_type=jnp.float32,
        )
        if first:
            part[pl.ds(r, n), :] = lanes
            acc[pl.ds(r, n), :] = value
        else:
            part[pl.ds(r, n), :] = part[pl.ds(r, n), :] * scale + lanes
            acc[pl.ds(r, n), :] = acc[pl.ds(r, n), :] * scale[:, :1] + value

    def work(units):
        pending = None
        for before, unit in units:
            if before is not None:
                before()
            s = score(*unit[:4])
            if pending is not None:
                absorb(*pending)
            pending = (s, *unit)
        absorb(*pending)

    def inner(a, na, b, nb):
        return lax.dot_general(
            rows[pl.ds(a, na), :],
            rows[pl.ds(b, nb), :],
            (((1,), (1,)), ((), ())),
            preferred_element_type=jnp.float32,
        )

    def other(slot):
        return base[slot] + size[slot]

    pl.semaphore_wait(barrier, len(nbr))
    boundary(0)
    load_rows.wait()
    load_own.wait()
    load_reach.wait()
    local, ghost, every = (0, count), (count, 2 * HALO), (0, total_rows)
    work([(None, (*local, 0, block, True))])
    launch(SECOND)
    band[:, pl.ds(0, count)] = inner(0, count, 0, count)
    for slot in range(1, 4):
        boundary(slot)
        shares[slot - 1].wait_recv()
        work([(None, (*local, other(slot - 1), size[slot - 1] + size[slot], False))])
    boundary(4)
    for copy in halo:
        copy.wait_recv()
    shares[3].wait_recv()
    work(
        [
            (None, (*local, other(3), size[3], False)),
            (None, (*ghost, 0, 4 * block, True)),
            (None, (*ghost, 4 * block, base[4] - 4 * block, False)),
            (shares[4].wait_recv, (*every, base[4], 2 * size[4], False)),
        ]
    )
    band[pl.ds(0, HALO), pl.ds(count, HALO)] = inner(0, HALO, count, HALO)
    band[pl.ds(count - HALO, HALO), pl.ds(count + HALO, HALO)] = inner(
        count - HALO, HALO, count + HALO, HALO
    )
    boundary(5)

    column = lax.broadcasted_iota(jnp.int32, (HALO, total_rows), 1)
    place_of = column - jnp.where(
        column < count, 0, jnp.where(column < count + HALO, count + HALO, HALO)
    )
    row = lax.broadcasted_iota(jnp.int32, (HALO, total_rows), 0)
    for start in range(0, count, HALO):
        width_of = jnp.broadcast_to(reach[pl.ds(start, HALO)][None, :], (HALO, HALO)).T[:, :1]
        offset = place_of - (row + start)
        inside = (jnp.abs(offset) <= width_of) & (offset != 0)
        b = jnp.where(inside, band[pl.ds(start, HALO), :] * (1.0 / width**0.5), jnp.float32(-1e30))
        highest = jnp.max(b, axis=1, keepdims=True)
        expo = jnp.where(inside, jnp.exp(b - highest), jnp.float32(0.0))
        mix[pl.ds(start, HALO), :] = (expo / jnp.sum(expo, axis=1, keepdims=True)).astype(
            jnp.bfloat16
        )

    def shared(group, boundaries=()):
        def wait():
            for slot in boundaries:
                boundary(slot)
            shares[group].wait_recv()

        return wait

    work(
        [
            (shared(5), (*every, base[5], 2 * size[5], False)),
            (shared(6), (*every, base[6], 2 * size[6], False)),
            (shared(7, (6, 7)), (*every, base[7], 2 * size[7], False)),
            (None, (*every, base[8], size[8], False)),
            (shared(8), (*every, other(8), size[8], False)),
        ]
    )

    total = jnp.sum(part[...], axis=1, keepdims=True)
    assigned[...] = (acc[...] * (1.0 / total)).astype(jnp.bfloat16)
    log_total = peak[pl.ds(0, count), :1] * gain + jnp.log(total[:count])
    for start in range(0, count, HALO):
        turned = jnp.broadcast_to(log_total[start : start + HALO], (HALO, HALO)).T
        lse[pl.ds(start, HALO)] = turned[0]
    for r, n, c in ((0, count - HALO, 0), (count - HALO, HALO, HALO)):
        columns = pl.ds(c, count + HALO) if c == 0 else pl.ds(c, total_rows - c)
        out[pl.ds(r, n), :] = jnp.dot(
            mix[pl.ds(r, n), columns], assigned[columns, :], preferred_element_type=jnp.float32
        ).astype(jnp.bfloat16)
    for copy in copies + shares + halo:
        copy.wait_send()


def shards(embed, centroids, reach):
    count, width = embed.shape
    block = centroids.shape[0]
    total = count + 2 * HALO
    table = block * lax.axis_size("grp")
    vmem = pl.BlockSpec(memory_space=pltpu.VMEM)
    hbm = pl.BlockSpec(memory_space=pltpu.HBM)
    smoothed, log_total = pl.pallas_call(
        kernel,
        out_shape=(
            jax.ShapeDtypeStruct((count, width), jnp.bfloat16),
            jax.ShapeDtypeStruct((count,), jnp.float32),
        ),
        in_specs=[hbm, hbm, hbm],
        out_specs=(vmem, vmem),
        scratch_shapes=[
            pltpu.VMEM((total, width), jnp.bfloat16),
            pltpu.VMEM((table, width), jnp.bfloat16),
            pltpu.VMEM((total, width), jnp.float32),
            pltpu.VMEM((total, 128), jnp.float32),
            pltpu.VMEM((total, 128), jnp.float32),
            pltpu.VMEM((count, total), jnp.float32),
            pltpu.VMEM((count, total), jnp.bfloat16),
            pltpu.VMEM((total, width), jnp.bfloat16),
            pltpu.VMEM((count,), jnp.int32),
            pltpu.SemaphoreType.DMA((len(SENDS),)),
            pltpu.SemaphoreType.DMA((len(SENDS),)),
            pltpu.SemaphoreType.DMA((len(GROUPS) + 1,)),
            pltpu.SemaphoreType.DMA((len(GROUPS) + 1,)),
            pltpu.SemaphoreType.DMA((2,)),
            pltpu.SemaphoreType.DMA((2,)),
            pltpu.SemaphoreType.DMA((3,)),
        ],
        compiler_params=pltpu.CompilerParams(
            collective_id=0, has_side_effects=True, vmem_limit_bytes=48 * 2**20
        ),
        cost_estimate=pl.CostEstimate(
            flops=4 * total * table * width, bytes_accessed=8 * 2**20, transcendentals=total * table
        ),
    )(*(pltpu.with_memory_space_constraint(a, pltpu.HBM) for a in (embed, centroids, reach)))
    return smoothed, log_total


def solution(mesh):
    return jax.shard_map(
        shards,
        mesh=mesh,
        in_specs=(P(("grp", "rng"), None), P("grp", None), P(("grp", "rng"))),
        out_specs=(P(("grp", "rng"), None), P(("grp", "rng"))),
        check_vma=False,
    )
```

time: 54.1 us -> 48.1 us (0.89)
  Pallas kernels: 48.7 us -> 45.9 us
  local copies, waits for them, and re-layouts: 3.84 us -> 1.46 us
  other arithmetic: 0.73 us -> 0 us
    pallas_call x1, Pallas kernels: 48.7 us -> 45.9 us  [shards(): pl.pallas_call(kernel, out_shape=(jax.ShapeDtypeStruct((count, width), jn...]
    unnamed x5 -> x2, local copies, waits for them, and re-layouts: 3.05 us -> 1.46 us
    broadcast_in_dim x1 -> x0, local copies, waits for them, and re-layouts: 0.79 us -> none  [shards(): reach[:, None]]
    pallas_call x1 -> x0, other arithmetic: 0.73 us -> none  [shards(): pl.pallas_call(kernel, out_shape=(jax.ShapeDtypeStruct((count, width), jn...]
where the time goes in v2:
time: 48.1 us; the launch traced here: 48 us
  Pallas kernels  45.9 us (95%)
  local copies, waits for them, and re-layouts  1.46 us (3%)
  between operations  0.64 us (1%)
    pallas_call x1, Pallas kernels, shards(): pl.pallas_call(kernel, out_shape=(jax.ShapeDtypeStruct((count, width), jn...  45.9 us
    unnamed x2, local copies, waits for them, and re-layouts  1.46 us

profile of v2, /device:TPU:1, one launch (start us, length us, event | category | flops | bytes accessed | tf_op | source)
XLA Modules:
  0.0 48.0 jit_solution(1877306032448075837)
XLA Ops:
  0.6 45.9 %shard_map.50 = (bf16[384,1024]{1,0:T(8,128)(2,1)S(1)}, f32[384]{0:T(512)S(1)}) custom-call(bf16[384,1024]{1,0:T(8,128)(2,1)} %embed.1, bf16[256,1024]{1,0:T(8,128)(2,1)} %cent.1, s32[384]{0:T(512)} %reach_in.1), custom_call_target="tpu_custom_call" | custom-call | flops 10737418240 | bytes 8388608 | tf_op jit(solution)/shard_map/pallas_call | solution.py:311
  46.6 0.9 %copy.7 = bf16[384,1024]{1,0:T(8,128)(2,1)} copy(bf16[384,1024]{1,0:T(8,128)(2,1)S(1)} %get-tuple-element.4) | data formatting | bytes 1572864
  47.4 0.6 %copy.8 = f32[384]{0:T(512)} copy(f32[384]{0:T(512)S(1)} %get-tuple-element.5) | data formatting | bytes 3072

commit v3 on v2

--- a/solution.py
+++ b/solution.py
@@ -176,7 +176,7 @@
             preferred_element_type=jnp.float32,
         )
 
-    def absorb(s, r, n, c, k, first):
+    def absorb(s, r, n, c, k, first, final=False):
         top = jnp.broadcast_to(jnp.max(s, axis=1, keepdims=True), (n, 128))
         if not first:
             old = peak[pl.ds(r, n), :]
@@ -192,7 +192,14 @@
             table[pl.ds(c, k), :],
             preferred_element_type=jnp.float32,
         )
-        if first:
+        if final:
+            total = jnp.sum(part[pl.ds(r, n), :] * scale + lanes, axis=1, keepdims=True)
+            part[pl.ds(r, n), :] = jnp.broadcast_to(total, (n, 128))
+            inverse = 1.0 / total
+            assigned[pl.ds(r, n), :] = (
+                (acc[pl.ds(r, n), :] * scale[:, :1] + value) * inverse
+            ).astype(jnp.bfloat16)
+        elif first:
             part[pl.ds(r, n), :] = lanes
             acc[pl.ds(r, n), :] = value
         else:
@@ -280,18 +287,14 @@
         [
             (shared(5), (*every, base[5], 2 * size[5], False)),
             (shared(6), (*every, base[6], 2 * size[6], False)),
-            (shared(7, (6, 7)), (*every, base[7], 2 * size[7], False)),
-            (None, (*every, base[8], size[8], False)),
-            (shared(8), (*every, other(8), size[8], False)),
+            (shared(7, (6, 7)), (*every, base[7], 2 * size[7] + size[8], False)),
+            (shared(8), (*every, other(8), size[8], False, True)),
         ]
     )
 
-    total = jnp.sum(part[...], axis=1, keepdims=True)
-    assigned[...] = (acc[...] * (1.0 / total)).astype(jnp.bfloat16)
-    log_total = peak[pl.ds(0, count), :1] * gain + jnp.log(total[:count])
     for start in range(0, count, HALO):
-        turned = jnp.broadcast_to(log_total[start : start + HALO], (HALO, HALO)).T
-        lse[pl.ds(start, HALO)] = turned[0]
+        here = pl.ds(start, HALO)
+        lse[here] = (peak[here, :] * gain + jnp.log(part[here, :])).T[0]
     for r, n, c in ((0, count - HALO, 0), (count - HALO, HALO, HALO)):
         columns = pl.ds(c, count + HALO) if c == 0 else pl.ds(c, total_rows - c)
         out[pl.ds(r, n), :] = jnp.dot(

time: 48.1 us -> 47.6 us (0.990)
  Pallas kernels: 45.9 us -> 45.4 us
    pallas_call x1, Pallas kernels: 45.9 us -> 45.4 us  [shards(): pl.pallas_call(kernel, out_shape=(jax.ShapeDtypeStruct((count, width), jn...]
where the time goes in v3:
time: 47.6 us; the launch traced here: 47.5 us
  Pallas kernels  45.4 us (95%)
  local copies, waits for them, and re-layouts  1.46 us (3%)
  between operations  0.64 us (1%)
    pallas_call x1, Pallas kernels, shards(): pl.pallas_call(kernel, out_shape=(jax.ShapeDtypeStruct((count, width), jn...  45.4 us
    unnamed x2, local copies, waits for them, and re-layouts  1.46 us

profile of v3, /device:TPU:1, one launch (start us, length us, event | category | flops | bytes accessed | tf_op | source)
XLA Modules:
  0.0 47.5 jit_solution(10162804595871219309)
XLA Ops:
  0.6 45.4 %shard_map.50 = (bf16[384,1024]{1,0:T(8,128)(2,1)S(1)}, f32[384]{0:T(512)S(1)}) custom-call(bf16[384,1024]{1,0:T(8,128)(2,1)} %embed.1, bf16[256,1024]{1,0:T(8,128)(2,1)} %cent.1, s32[384]{0:T(512)} %reach_in.1), custom_call_target="tpu_custom_call" | custom-call | flops 10737418240 | bytes 8388608 | tf_op jit(solution)/shard_map/pallas_call | solution.py:314
  46.1 0.9 %copy.7 = bf16[384,1024]{1,0:T(8,128)(2,1)} copy(bf16[384,1024]{1,0:T(8,128)(2,1)S(1)} %get-tuple-element.4) | data formatting | bytes 1572864
  46.9 0.6 %copy.8 = f32[384]{0:T(512)} copy(f32[384]{0:T(512)S(1)} %get-tuple-element.5) | data formatting | bytes 3072

commit v4 on v3

--- a/solution.py
+++ b/solution.py
@@ -259,21 +259,29 @@
     )
     boundary(5)
 
-    column = lax.broadcasted_iota(jnp.int32, (HALO, total_rows), 1)
-    place_of = column - jnp.where(
-        column < count, 0, jnp.where(column < count + HALO, count + HALO, HALO)
-    )
-    row = lax.broadcasted_iota(jnp.int32, (HALO, total_rows), 0)
-    for start in range(0, count, HALO):
-        width_of = jnp.broadcast_to(reach[pl.ds(start, HALO)][None, :], (HALO, HALO)).T[:, :1]
-        offset = place_of - (row + start)
-        inside = (jnp.abs(offset) <= width_of) & (offset != 0)
-        b = jnp.where(inside, band[pl.ds(start, HALO), :] * (1.0 / width**0.5), jnp.float32(-1e30))
-        highest = jnp.max(b, axis=1, keepdims=True)
-        expo = jnp.where(inside, jnp.exp(b - highest), jnp.float32(0.0))
-        mix[pl.ds(start, HALO), :] = (expo / jnp.sum(expo, axis=1, keepdims=True)).astype(
-            jnp.bfloat16
-        )
+    tile = (HALO, HALO)
+    ahead = lax.broadcasted_iota(jnp.int32, tile, 1) - lax.broadcasted_iota(jnp.int32, tile, 0)
+    n_tile = count // HALO
+    columns_of = {-1: count, n_tile: count + HALO, **{i: i * HALO for i in range(n_tile)}}
+    for t in range(n_tile):
+        here = pl.ds(t * HALO, HALO)
+        reach_of = jnp.broadcast_to(reach[here][None, :], tile).T
+        values, masks = [], []
+        for step in (-1, 0, 1):
+            offset = ahead + step * HALO
+            inside = (jnp.abs(offset) <= reach_of) & (offset != 0)
+            value = band[here, pl.ds(columns_of[t + step], HALO)] * (1.0 / width**0.5)
+            values.append(jnp.where(inside, value, jnp.float32(-1e30)))
+            masks.append(inside)
+        highest = jnp.max(jnp.maximum(jnp.maximum(*values[:2]), values[2]), axis=1, keepdims=True)
+        expo = [
+            jnp.where(inside, jnp.exp(value - highest), jnp.float32(0.0))
+            for value, inside in zip(values, masks)
+        ]
+        inverse = 1.0 / jnp.sum(expo[0] + expo[1] + expo[2], axis=1, keepdims=True)
+        mix[here, :] = jnp.zeros((HALO, total_rows), jnp.bfloat16)
+        for step, e in zip((-1, 0, 1), expo):
+            mix[here, pl.ds(columns_of[t + step], HALO)] = (e * inverse).astype(jnp.bfloat16)
 
     def shared(group, boundaries=()):
         def wait():

time: 47.6 us -> 47.6 us (level)
  no operation moved by 1% of the time
where the time goes in v4:
time: 47.6 us; the launch traced here: 47.5 us
  Pallas kernels  45.4 us (95%)
  local copies, waits for them, and re-layouts  1.46 us (3%)
  between operations  0.64 us (1%)
    pallas_call x1, Pallas kernels, shards(): pl.pallas_call(kernel, out_shape=(jax.ShapeDtypeStruct((count, width), jn...  45.4 us
    unnamed x2, local copies, waits for them, and re-layouts  1.46 us

profile of v4, /device:TPU:1, one launch (start us, length us, event | category | flops | bytes accessed | tf_op | source)
XLA Modules:
  0.0 47.5 jit_solution(5706723079576182352)
XLA Ops:
  0.6 45.4 %shard_map.50 = (bf16[384,1024]{1,0:T(8,128)(2,1)S(1)}, f32[384]{0:T(512)S(1)}) custom-call(bf16[384,1024]{1,0:T(8,128)(2,1)} %embed.1, bf16[256,1024]{1,0:T(8,128)(2,1)} %cent.1, s32[384]{0:T(512)} %reach_in.1), custom_call_target="tpu_custom_call" | custom-call | flops 10737418240 | bytes 8388608 | tf_op jit(solution)/shard_map/pallas_call | solution.py:322
  46.0 0.9 %copy.7 = bf16[384,1024]{1,0:T(8,128)(2,1)} copy(bf16[384,1024]{1,0:T(8,128)(2,1)S(1)} %get-tuple-element.4) | data formatting | bytes 1572864
  46.9 0.6 %copy.8 = f32[384]{0:T(512)} copy(f32[384]{0:T(512)S(1)} %get-tuple-element.5) | data formatting | bytes 3072
